TPU v7x, 32 devices: a whole 2x2x4 slice. The times are simulated.
32 devices in a mesh: wide: 8 (over y, x, core), narrow: 4 (over z).
Axes of the slice: x: 2, y: 2, z: 4, core: 2. Of those that a mesh axis runs over, the one named last changes fastest.
Arguments:
- diag_blocks: float32 [8, 512, 512], P('wide'), as said below
- row_panel: bfloat16 [8, 1024, 512], P('wide', 'narrow'), may hold values from -6 to 6
- col_panel: bfloat16 [8, 1024, 512], P('wide', 'narrow'), may hold values from -6 to 6
- row_tiles: int32 [8, 4], P('wide'), may hold values from 0 to 7, as said below
- col_mask: int32 [8, 4], P('wide', 'narrow'), may hold values 0 or 1
- slot_tile: int32 [8], replicated, may hold values from 0 to 7, each once
- trailing: float32 [2048, 1024], P('wide', 'narrow'), may hold values from -6 to 6
Outputs:
- schur_block: float32 [2048, 1024], P('wide', 'narrow')
Inputs may be any that keep to these rules, and one draw needn't show every extreme that they name: `row_tiles`: the 4 ids of one supernode are distinct. `slot_tile`: a permutation of the row-tile ids. `diag_blocks`: each block is symmetric and positive definite, its smallest eigenvalue at least 30.
All inputs are finite; a program needn't handle non-finite values. No bound on the sum of `col_mask` on one device may be relied on, other than what follows from the above.
Results may differ from a plain program's by a relative error of at most 0.013.
Values may be sent and summed in bfloat16 or wider, within the bound.
A program may use at most 64 MiB of HBM per device.

v0:
```python
import jax
import jax.numpy as jnp
from jax import lax
from jax.sharding import PartitionSpec as P


def solve_single(panel, factor_low):
    solved = lax.linalg.triangular_solve(
        factor_low, panel.astype(jnp.float32), left_side=False, lower=True, transpose_a=True
    )
    return solved.astype(jnp.bfloat16)


def solve_rows(panel, factor_low):
    return jax.vmap(solve_single)(panel, factor_low)


def local(diag_blocks, row_panel, col_panel, row_tiles, col_mask, slot_tile, trailing):
    tile_rows = col_panel.shape[1]
    slot_count = slot_tile.shape[0]
    factor_low = jax.vmap(jnp.linalg.cholesky)(diag_blocks)
    col_factor = solve_rows(col_panel, factor_low)
    positions = jnp.arange(slot_count, dtype=jnp.int32)
    perm_table = (slot_tile[None, :] == positions[:, None]).astype(jnp.float32)
    tile_onehot = (row_tiles[:, :, None] == positions[None, None, :]).astype(jnp.float32)
    placing = jnp.einsum("sai,ip->sap", tile_onehot, perm_table, precision=lax.Precision.HIGHEST)
    placing = placing * col_mask.astype(jnp.float32)[:, :, None]
    row_factor = solve_rows(row_panel, factor_low)
    products = jnp.einsum(
        "sra,sca->src",
        lax.all_gather(row_factor, "narrow", axis=1, tiled=True),
        col_factor,
        preferred_element_type=jnp.float32,
    )
    supernodes = products.shape[0]
    blocks = products.reshape(supernodes, products.shape[1] // tile_rows, tile_rows, tile_rows)
    gathered_sum = jnp.einsum("sap,saij->pij", placing, blocks, precision=lax.Precision.HIGHEST)
    summed = lax.psum_scatter(
        gathered_sum.reshape(slot_count * tile_rows, tile_rows).astype(jnp.bfloat16),
        "wide",
        scatter_dimension=0,
        tiled=True,
    ).astype(jnp.float32)
    return trailing - summed


def solution(mesh):
    placed = (
        P("wide", None, None),
        P("wide", "narrow", None),
        P("wide", "narrow", None),
        P("wide", None),
        P("wide", "narrow"),
        P(),
        P("wide", "narrow"),
    )
    return jax.shard_map(
        local, mesh=mesh, in_specs=placed, out_specs=P("wide", "narrow"), check_vma=False
    )
```

profile of v0, /device:TPU:0, one launch (start us, length us, event | category | flops | bytes accessed | tf_op | source)
XLA Modules:
  0.0 225.6 jit_solution(14907908070372686337)
XLA Ops:
  6.5 1.6 copy.9
  8.5 11.7 %custom-call.34 = f32[1,128,128]{2,1,0:T(8,128)S(1)} custom-call(f32[1,128,128]{2,1,0:T(8,128)S(1)} %cholesky.267), custom_call_target="Cholesky" | custom-call | tf_op jit(solution)/shard_map/vmap(jit(cholesky))/cholesky | solution.py:21
  20.2 9.8 %custom-call.35 = f32[1,1,128,128]{2,3,1,0:T(8,128)S(1)} custom-call(f32[1,1,128,128]{3,2,1,0:T(8,128)S(1)} %get-tuple-element.41), custom_call_target="InvertDiagBlocksLowerTriangular" | custom-call | tf_op jit(solution)/shard_map/vmap(jit(cholesky))/cholesky | solution.py:21
  30.8 11.7 %custom-call.36 = f32[1,128,128]{2,1,0:T(8,128)S(1)} custom-call(f32[1,128,128]{2,1,0:T(8,128)S(1)} %cholesky.271), custom_call_target="Cholesky" | custom-call | tf_op jit(solution)/shard_map/vmap(jit(cholesky))/cholesky | solution.py:21
  42.6 10.0 %custom-call.37 = f32[1,1,128,128]{2,3,1,0:T(8,128)S(1)} custom-call(f32[1,1,128,128]{3,2,1,0:T(8,128)S(1)} %get-tuple-element.38), custom_call_target="InvertDiagBlocksLowerTriangular" | custom-call | tf_op jit(solution)/shard_map/vmap(jit(cholesky))/cholesky | solution.py:21
  53.2 11.7 %custom-call.38 = f32[1,128,128]{2,1,0:T(8,128)S(1)} custom-call(f32[1,128,128]{2,1,0:T(8,128)S(1)} %cholesky.276), custom_call_target="Cholesky" | custom-call | tf_op jit(solution)/shard_map/vmap(jit(cholesky))/cholesky | solution.py:21
  65.0 0.7 compare_reduce_fusion.1
  65.7 9.8 %custom-call.39 = f32[1,1,128,128]{2,3,1,0:T(8,128)S(1)} custom-call(f32[1,1,128,128]{3,2,1,0:T(8,128)S(1)} %get-tuple-element.35), custom_call_target="InvertDiagBlocksLowerTriangular" | custom-call | tf_op jit(solution)/shard_map/vmap(jit(cholesky))/cholesky | solution.py:21
  76.1 11.7 %custom-call.40 = f32[1,128,128]{2,1,0:T(8,128)S(1)} custom-call(f32[1,128,128]{2,1,0:T(8,128)S(1)} %fusion.16), custom_call_target="Cholesky" | custom-call | tf_op jit(solution)/shard_map/vmap(jit(cholesky))/cholesky | solution.py:21
  87.9 0.6 compare_reduce_fusion
  88.5 0.7 compare_reduce_fusion.2
  92.1 8.1 %while.4 = (s32[]{:T(128)}, f32[1,512,512]{2,1,0:T(8,128)S(1)}, s32[4,2]{0,1:T(2,128)S(1)}, f32[4,1,128,128]{3,2,1,0:T(8,128)S(1)}, s32[]{:T(128)}) while((s32[]{:T(128)}, f32[1,512,512]{2,1,0:T(8,128)S(1)}, s32[4,2]{0,1:T(2,128)S(1)}, f32[4,1,128,128]{3,2,1,0:T(8,128)S(1)}, s32[]{:T(128)}) %tuple.32), condition=%wide.while_cond, body=%wide.while_body.sunk | while | flops 2 | bytes 131181 | solution.py:8
  92.2 0.6 fusion.61
  92.8 1.3 bitcast_dynamic-update-slice_fusion.2
  94.2 0.6 fusion.61
  94.8 1.3 bitcast_dynamic-update-slice_fusion.2
  96.3 0.6 fusion.61
  96.9 1.3 bitcast_dynamic-update-slice_fusion.2
  98.3 0.6 fusion.61
  98.9 1.3 bitcast_dynamic-update-slice_fusion.2
  100.2 39.3 %custom-call.42 = f32[1,4,128,128]{2,3,1,0:T(8,128)S(1)} custom-call(f32[1,4,128,128]{3,2,1,0:T(8,128)S(1)} %bitcast.230), custom_call_target="InvertDiagBlocksLowerTriangular" | custom-call | tf_op jit(solution)/shard_map/vmap()/triangular_solve/custom-call.3 | solution.py:8
  140.7 0.6 fusion.8
  141.6 0.8 fusion.12
  142.8 0.7 maximum_convert_fusion
  145.6 0.6 fusion.10
  146.5 0.8 fusion.14
  147.6 29.0 %all-gather.2.cloned.1.call-done = bf16[1,1024,512]{1,2,0:T(8,128)(2,1)} async-done(((bf16[1,256,512]{1,2,0:T(8,128)(2,1)}), bf16[1,1024,512]{1,2,0:T(8,128)(2,1)}) %all-gather.2.cloned.1.call-update) | async-done | bytes 1048592 | tf_op jit(solution)/shard_map/all_gather | solution.py:31
  176.6 1.5 copy.13
  178.5 2.8 %convolution_convert_fusion = bf16[8,256,256]{2,0,1:T(8,128)(2,1)S(1)} fusion(f32[4,8,1]{1,0,2:T(4,128)S(1)} %fusion.17, f32[4,256,256]{2,1,0:T(8,128)S(1)} %fusion.29), kind=kOutput, calls=%fused_computation.2 | convolution fusion | flops 25690112 | bytes 2097280 | tf_op jit(solution)/shard_map/sap,saij->pij/dot_general | solution.py:37
  181.4 1.2 copy.10
  182.6 34.5 %reduce-scatter.2.cloned.1.call-done = bf16[256,256]{1,0:T(8,128)(2,1)} async-done(((bf16[2048,256]{1,0:T(8,128)(2,1)}), bf16[256,256]{1,0:T(8,128)(2,1)}) %reduce-scatter.2.cloned.1.call-update) | async-done | bytes 131088 | tf_op jit(solution)/shard_map/reduce_scatter | solution.py:38
  217.1 1.6 convert_subtract_fusion
  (53 shorter events, 7.2 us)
Async XLA Ops:
  6.5 170.1 %all-gather.2.cloned.1.call-start = ((), (), s32[]{:S(2)}) async-start(), calls=%async_computation.1 | async-start | bytes 1310720 | tf_op jit(solution)/shard_map/all_gather | solution.py:31
  6.5 1.7 copy-start
  91.7 47.9 %copy-start.1 = (bf16[1,256,512]{2,1,0:T(8,128)(2,1)S(1)}, bf16[1,256,512]{2,1,0:T(8,128)(2,1)}, u32[]{:S(2)}) copy-start(bf16[1,256,512]{2,1,0:T(8,128)(2,1)} %param.10) | copy-start | bytes 786436
  141.6 2.0 copy-start.2
  142.5 1.9 copy-start.4
  142.5 1.9 copy-start.5
  143.6 73.6 %reduce-scatter.2.cloned.1.call-start = ((), (), s32[]{:S(2)}) async-start(), calls=%async_computation.2 | async-start | bytes 1179648 | tf_op jit(solution)/shard_map/reduce_scatter | solution.py:38
  182.6 34.6 %copy-start.3 = (f32[256,256]{1,0:T(8,128)S(1)}, f32[256,256]{1,0:T(8,128)}, u32[]{:S(2)}) copy-start(f32[256,256]{1,0:T(8,128)} %param.15) | copy-start | bytes 786436
Sparse Core Ops, SparseCore 0:
  143.7 32.8 all-gather.1
  182.7 34.3 reduce-scatter.1
where the time goes:
time: 226 us
  other arithmetic  121 us (54%)
  waiting for transfers between devices  63.5 us (28%)
  between operations  16.9 us (7%)
  local copies, waits for them, and re-layouts  12.6 us (6%)
  matrix products  11.4 us (5%)
    another operation x14, other arithmetic, local(): factor_low = jax.vmap(jnp.linalg.cholesky)(diag_blocks)  78.6 us
    another operation x4, other arithmetic, solve_single(): lax.linalg.triangular_solve(factor_low, panel.astype(jnp.float32), left_s...  39.7 us
    reduce_scatter x1, waiting for transfers between devices, local(): lax.psum_scatter(gathered_sum.reshape(slot_count * tile_rows, tile_rows)....  34.5 us
    all_gather x1, waiting for transfers between devices, local(): lax.all_gather(row_factor, 'narrow', axis=1, tiled=True)  29 us
    another operation x13, local copies, waits for them, and re-layouts, solve_single(): lax.linalg.triangular_solve(factor_low, panel.astype(jnp.float32), left_s...  8.06 us
    another operation x14, matrix products, solve_single(): lax.linalg.triangular_solve(factor_low, panel.astype(jnp.float32), left_s...  6.13 us
  transfers between devices with their start and end apart: 2, of which 2 were waited for; matrix products, arithmetic and copies ran while one was open for 1% of the time, Pallas kernels for 0%

commit v1 on v0

v1 whole, which is shorter than its diff:
```python
import functools

import jax
import jax.numpy as jnp
from jax import lax
from jax.experimental import pallas as pl
from jax.experimental.pallas import tpu as pltpu
from jax.sharding import PartitionSpec as P

F32 = jnp.float32
BF16 = jnp.bfloat16
MESH = pl.DeviceIdType.MESH
LEAST = 30.0
ENOUGH = 1e-3
VMEM_LIMIT = 48 * 1024 * 1024


def mm(a, b):
    return jnp.dot(a, b, preferred_element_type=F32)


def split(a):
    high = a.astype(BF16)
    return high, (a - high.astype(F32)).astype(BF16)


def eliminate(diag_ref, panel_ref, solved_ref, low_ref, sides_ref):
    n = diag_ref.shape[0]
    low_ref[...] = diag_ref[...]
    sides_ref[...] = panel_ref[...].astype(F32).T
    lane = lax.broadcasted_iota(jnp.int32, (1, n), 1)
    place = lax.broadcasted_iota(jnp.int32, (n, 1), 0)

    def pivot(k, carry):
        row = low_ref[pl.ds(k, 1), :]
        side = sides_ref[pl.ds(k, 1), :]
        scale = 1.0 / jnp.sum(jnp.where(lane == k, row, 0.0), axis=1, keepdims=True)
        col = jnp.sum(jnp.where(lane == k, low_ref[...], 0.0), axis=1, keepdims=True)
        col = jnp.where(place == k, 0.0, col)
        row, side = row * scale, side * scale
        low_ref[...] = low_ref[...] - col * row
        sides_ref[...] = sides_ref[...] - col * side
        low_ref[pl.ds(k, 1), :] = row
        sides_ref[pl.ds(k, 1), :] = side
        return carry

    lax.fori_loop(0, n, pivot, 0)
    solved_ref[...] = sides_ref[...].T


def solve_kernel(diag_ref, panel_ref, high_ref, low_out_ref, e_ref, x_ref, y_ref, low_ref, sides_ref):
    n = diag_ref.shape[0]
    diag = diag_ref[...]
    eye = (
        lax.broadcasted_iota(jnp.int32, (n, n), 0) == lax.broadcasted_iota(jnp.int32, (n, n), 1)
    ).astype(F32)
    most = jnp.max(jnp.sum(jnp.abs(diag), axis=1))
    scale = 2.0 / (LEAST + most)
    gap = (most - LEAST) / (most + LEAST)
    e = eye - scale * diag
    gain = 2.0 / (2.0 - gap * gap)
    x_ref[...] = (gain * scale) * (eye + e)
    eb = e.astype(BF16)
    e_ref[...] = (1.0 - gain) * eye + gain * mm(eb, eb)
    gap = gap * gap * 0.5 * gain

    def newton(carry):
        gap, step = carry
        gain = 2.0 / (2.0 - gap * gap)
        eb = e_ref[...].astype(BF16)
        x = x_ref[...]
        x_ref[...] = gain * (x + mm(x.astype(BF16), eb))
        e_ref[...] = (1.0 - gain) * eye + gain * mm(eb, eb)
        return gap * gap * 0.5 * gain, step + 1

    lax.while_loop(lambda c: (c[0] > 0.15) & (c[1] < 16), newton, (gap, jnp.int32(0)))
    eb = e_ref[...].astype(BF16)
    x = x_ref[...]
    inverse = (x + mm(x.astype(BF16), eb)).astype(BF16)

    panel = panel_ref[...]
    size = jnp.sum(panel.astype(F32) ** 2)
    diag_high, diag_low = split(diag)
    y_ref[...] = mm(panel, inverse)

    def refine(carry):
        _, step = carry
        y = y_ref[...]
        y_high, y_low = split(y)
        rest = panel.astype(F32) - mm(y_high, diag_high) - mm(y_high, diag_low) - mm(y_low, diag_high)
        y_ref[...] = y + mm(rest.astype(BF16), inverse)
        return jnp.sum(rest * rest), step + 1

    def unfinished(carry):
        return jnp.logical_not(carry[0] <= ENOUGH * ENOUGH * size)

    left, _ = lax.while_loop(
        lambda c: unfinished(c) & (c[1] < 8), refine, refine((F32(0), jnp.int32(0)))
    )

    @pl.when(unfinished((left, 0)))
    def _():
        eliminate(diag_ref, panel_ref, y_ref, low_ref, sides_ref)

    high_ref[...], low_out_ref[...] = split(y_ref[...])


def solve(diag, panel):
    n, rows = diag.shape[0], panel.shape[0]
    return pl.pallas_call(
        solve_kernel,
        out_shape=[jax.ShapeDtypeStruct((rows, n), BF16)] * 2,
        in_specs=[pl.BlockSpec(memory_space=pltpu.VMEM)] * 2,
        out_specs=[pl.BlockSpec(memory_space=pltpu.VMEM)] * 2,
        scratch_shapes=[
            pltpu.VMEM((n, n), F32),
            pltpu.VMEM((n, n), F32),
            pltpu.VMEM((rows, n), F32),
            pltpu.VMEM((n, n), F32),
            pltpu.VMEM((n, rows), F32),
        ],
        compiler_params=pltpu.CompilerParams(vmem_limit_bytes=VMEM_LIMIT),
        cost_estimate=pl.CostEstimate(
            flops=100 * n * n * n, bytes_accessed=4 * n * n, transcendentals=0
        ),
    )(diag, panel)


def update_kernel(wide, narrow, tiles, *refs):
    place_ref, weight_ref, high_ref, low_ref, trailing_ref = refs[:5]
    panel_refs = refs[5 : 5 + tiles]
    out_ref, products, acc, first_send, first_recv, sends, recvs, first_sems, sems = refs[5 + tiles :]
    bits = wide.bit_length() - 1
    size = out_ref.shape[0]
    half = size // 2
    me = lax.axis_index("wide")
    own_bit = [lax.rem(lax.div(me, 1 << b), 2) for b in range(bits)]

    def partner(b):
        return me + (1 - 2 * own_bit[b]) * (1 << b)

    def slot(r):
        return sum(
            ((1 - own_bit[b]) if (r >> b) & 1 else own_bit[b]) * (1 << b) for b in range(bits)
        )

    barrier = pltpu.get_barrier_semaphore()
    for b in range(bits):
        pl.semaphore_signal(barrier, inc=1, device_id={"wide": partner(b)}, device_id_type=MESH)

    dims = (((1,), (1,)), ((), ()))
    for k in range(tiles):
        panel = panel_refs[k][...]
        products[k] = lax.dot_general(
            panel, high_ref[...], dims, preferred_element_type=F32
        ) + lax.dot_general(panel, low_ref[...], dims, preferred_element_type=F32)
    pl.semaphore_wait(barrier, bits)

    def own(r):
        p = slot(r)
        return products[place_ref[p]] * weight_ref[p]

    def first_copy(i):
        return pltpu.make_async_remote_copy(
            src_ref=first_send.at[i],
            dst_ref=first_recv.at[i],
            send_sem=first_sems.at[0, i],
            recv_sem=first_sems.at[1, i],
            device_id={"wide": partner(0)},
            device_id_type=MESH,
        )

    for i in range(wide // 2):
        first_send[i] = own(2 * i + 1).astype(BF16)
        first_copy(i).start()
    for i in range(wide // 2):
        first_copy(i).wait_recv()
        acc[i] = own(2 * i) + first_recv[i].astype(F32)

    orders = [list(range(1, bits)), list(range(bits - 1, 0, -1))]
    left = [list(range(0, wide, 2)), list(range(0, wide, 2))]
    base = [0, 0]
    for step in range(bits - 1):
        copies = []
        for h in range(2):
            b = orders[h][step]
            gone = [r for r in left[h] if (r >> b) & 1]
            left[h] = [r for r in left[h] if not (r >> b) & 1]
            at = base[h]
            count = len(gone)
            for i, r in enumerate(gone):
                sends[h, at + i] = acc[r // 2, h * half : (h + 1) * half, :].astype(BF16)
            copy = pltpu.make_async_remote_copy(
                src_ref=sends.at[h, pl.ds(at, count)],
                dst_ref=recvs.at[h, pl.ds(at, count)],
                send_sem=sems.at[0, h, step],
                recv_sem=sems.at[1, h, step],
                device_id={"wide": partner(b)},
                device_id_type=MESH,
            )
            copy.start()
            copies.append((copy, [r - (1 << b) for r in gone], at))
            base[h] = at + count
        for h in range(2):
            copy, kept, at = copies[h]
            copy.wait()
            for i, r in enumerate(kept):
                acc[r // 2, h * half : (h + 1) * half, :] += recvs[h, at + i].astype(F32)
    for i in range(wide // 2):
        first_copy(i).wait_send()
    out_ref[...] = trailing_ref[...] - acc[0]


def update(wide, narrow, place, weight, high, low, trailing, panels):
    tiles = len(panels)
    rows, cols = trailing.shape
    bits = wide.bit_length() - 1
    vmem = pl.BlockSpec(memory_space=pltpu.VMEM)
    smem = pl.BlockSpec(memory_space=pltpu.SMEM)
    return pl.pallas_call(
        functools.partial(update_kernel, wide, narrow, tiles),
        out_shape=jax.ShapeDtypeStruct((rows, cols), F32),
        in_specs=[smem, smem] + [vmem] * (3 + tiles),
        out_specs=vmem,
        scratch_shapes=[
            pltpu.VMEM((tiles, rows, cols), F32),
            pltpu.VMEM((wide // 2, rows, cols), F32),
            pltpu.VMEM((wide // 2, rows, cols), BF16),
            pltpu.VMEM((wide // 2, rows, cols), BF16),
            pltpu.VMEM((2, wide // 2, rows // 2, cols), BF16),
            pltpu.VMEM((2, wide // 2, rows // 2, cols), BF16),
            pltpu.SemaphoreType.DMA((2, wide // 2)),
            pltpu.SemaphoreType.DMA((2, 2, bits)),
        ],
        compiler_params=pltpu.CompilerParams(
            collective_id=0, has_side_effects=True, vmem_limit_bytes=VMEM_LIMIT
        ),
    )(place, weight, high, low, trailing, *panels)


def local(wide, narrow, diag_blocks, row_panel, col_panel, row_tiles, col_mask, slot_tile, trailing):
    panel = row_panel[0]
    shifted = [panel]
    for d in range(1, narrow):
        shifted.append(lax.ppermute(panel, "narrow", [(i, (i + d) % narrow) for i in range(narrow)]))
    high, low = solve(diag_blocks[0], col_panel[0])
    own = lax.axis_index("narrow")
    hits = slot_tile[:, None] == row_tiles[0][None, :]
    distance = (own - jnp.arange(narrow, dtype=jnp.int32)) % narrow
    place = jnp.sum(jnp.where(hits, distance[None, :], 0), axis=1).astype(jnp.int32)
    weight = jnp.any(hits, axis=1).astype(F32) * col_mask[0, 0].astype(F32)
    return update(wide, narrow, place, weight, high, low, trailing, shifted)


def solution(mesh):
    placed = (
        P("wide", None, None),
        P("wide", "narrow", None),
        P("wide", "narrow", None),
        P("wide", None),
        P("wide", "narrow"),
        P(),
        P("wide", "narrow"),
    )
    return jax.shard_map(
        functools.partial(local, mesh.shape["wide"], mesh.shape["narrow"]),
        mesh=mesh,
        in_specs=placed,
        out_specs=P("wide", "narrow"),
        check_vma=False,
    )
```

time: 226 us -> 40.9 us (0.18)
  other arithmetic: 121 us -> 0.19 us
  waiting for transfers between devices: 63.5 us -> 13.2 us
  Pallas kernels: 0 us -> 17.1 us
  between operations: 16.9 us -> 0.71 us
  matrix products: 11.4 us -> 0 us
  local copies, waits for them, and re-layouts: 12.6 us -> 3.54 us
  starting transfers between devices: 0.04 us -> 6.06 us
    another operation x18 -> x0, other arithmetic: 118 us -> none  [the longest x14 78.6 us: local(): factor_low = jax.vmap(jnp.linalg.cholesky)(diag_blocks)]
    reduce_scatter x1 -> x0, waiting for transfers between devices: 34.5 us -> none  [local(): lax.psum_scatter(gathered_sum.reshape(slot_count * tile_rows, tile_rows)....]
    all_gather x1 -> x0, waiting for transfers between devices: 29 us -> none  [local(): lax.all_gather(row_factor, 'narrow', axis=1, tiled=True)]
    pallas_call x0 -> x2, Pallas kernels: none -> 17.1 us  [the longest x1 12.5 us: update(): pl.pallas_call(functools.partial(update_kernel, wide, narrow, tiles), out...]
    ppermute x0 -> x3, waiting for transfers between devices: none -> 13.2 us  [local(): lax.ppermute(panel, 'narrow', [(i, (i + d) % narrow) for i in range(narro...]
    another operation x18 -> x0, local copies, waits for them, and re-layouts: 9.69 us -> none  [the longest x13 8.06 us: solve_single(): lax.linalg.triangular_solve(factor_low, panel.astype(jnp.float32), left_s...]
    another operation x20 -> x0, matrix products: 8.01 us -> none  [the longest x14 6.13 us: solve_single(): lax.linalg.triangular_solve(factor_low, panel.astype(jnp.float32), left_s...]
    ppermute x0 -> x3, starting transfers between devices: none -> 6.06 us  [local(): lax.ppermute(panel, 'narrow', [(i, (i + d) % narrow) for i in range(narro...]
  transfers between devices with their start and end apart: 2 -> 3, of which waited for: 2 -> 1; matrix products, arithmetic and copies ran while one was open for 1% -> 0% of each run, Pallas kernels for 0% -> 11%
where the time goes in v1:
time: 40.9 us; the launch traced here: 40.8 us
  Pallas kernels  17.1 us (42%)
  waiting for transfers between devices  13.2 us (32%)
  starting transfers between devices  6.06 us (15%)
  local copies, waits for them, and re-layouts  3.54 us (9%)
  between operations  0.71 us (2%)
    ppermute x3, waiting for transfers between devices, local(): lax.ppermute(panel, 'narrow', [(i, (i + d) % narrow) for i in range(narro...  13.2 us
    pallas_call x1, Pallas kernels, update(): pl.pallas_call(functools.partial(update_kernel, wide, narrow, tiles), out...  12.5 us
    ppermute x3, starting transfers between devices, local(): lax.ppermute(panel, 'narrow', [(i, (i + d) % narrow) for i in range(narro...  6.06 us
    pallas_call x1, Pallas kernels, solve(): pl.pallas_call(solve_kernel, out_shape=[jax.ShapeDtypeStruct((rows, n), B...  4.63 us
    unnamed x13, local copies, waits for them, and re-layouts  3.54 us
  transfers between devices with their start and end apart: 3, of which 1 were waited for; matrix products, arithmetic and copies ran while one was open for 0% of the time, Pallas kernels for 11%

profile of v1, /device:TPU:0, one launch (start us, length us, event | category | flops | bytes accessed | tf_op | source)
XLA Modules:
  0.0 40.8 jit_solution(12786039899868959976)
XLA Ops:
  0.0 5.0 %collective-permute-start.2 = (bf16[256,512]{1,0:T(8,128)(2,1)}, bf16[256,512]{1,0:T(8,128)(2,1)S(1)}, u32[]{:S(2)}, u32[]{:S(2)}) collective-permute-start(bf16[256,512]{1,0:T(8,128)(2,1)} %bitcast.5), channel_id=1, source_target_pairs={{0,3},{1,0},{2,1},{3,2},{4,7},{5,4},{6,5},{7,6},{8,11},{9,8},{10,9... | collective-permute-start | bytes 786440 | tf_op jit(solution)/shard_map/ppermute | solution.py:245
  5.0 0.0 collective-permute-start.1
  5.1 1.0 %collective-permute-start = (bf16[256,512]{1,0:T(8,128)(2,1)}, bf16[256,512]{1,0:T(8,128)(2,1)S(1)}, u32[]{:S(2)}, u32[]{:S(2)}) collective-permute-start(bf16[256,512]{1,0:T(8,128)(2,1)} %bitcast.7), channel_id=1, source_target_pairs={{0,1},{1,2},{2,3},{3,0},{4,5},{5,6},{6,7},{7,4},{8,9},{9,10},{10,1... | collective-permute-start | bytes 786440 | tf_op jit(solution)/shard_map/ppermute | solution.py:245
  6.1 0.0 copy-start.2
  6.1 1.2 %copy-done.2 = f32[1,512,512]{2,1,0:T(8,128)S(1)} copy-done((f32[1,512,512]{2,1,0:T(8,128)S(1)}, f32[1,512,512]{2,1,0:T(8,128)}, u32[]{:S(2)}) %copy-start.2) | copy-done | bytes 1048600
  7.3 0.0 copy-start.3
  7.3 0.9 %copy-done.3 = bf16[1,256,512]{2,1,0:T(8,128)(2,1)S(1)} copy-done((bf16[1,256,512]{2,1,0:T(8,128)(2,1)S(1)}, bf16[1,256,512]{2,1,0:T(8,128)(2,1)}, u32[]{:S(2)}) %copy-start.3) | copy-done | bytes 262168
  8.3 0.0 copy-start
  8.3 0.0 copy-start.1
  8.3 4.6 %shard_map.73 = (bf16[256,512]{1,0:T(8,128)(2,1)S(1)}, bf16[256,512]{1,0:T(8,128)(2,1)S(1)}) custom-call(f32[512,512]{1,0:T(8,128)S(1)} %bitcast.9, bf16[256,512]{1,0:T(8,128)(2,1)S(1)} %bitcast.10), custom_call_target="tpu_custom_call" | custom-call | flops 13421772800 | bytes 1048576 | tf_op jit(solution)/shard_map/pallas_call | solution.py:110
  12.9 0.0 copy-start.4
  12.9 0.0 copy-start.5
  12.9 0.6 %copy-done.4 = s32[8]{0:T(128)S(1)} copy-done((s32[8]{0:T(128)S(1)}, s32[8]{0:T(128)}, u32[]{:S(2)}) %copy-start.4) | copy-done | bytes 56
  13.6 0.0 copy-done.5
  13.6 0.1 fusion.refs_0_
  13.7 0.1 compare_reduce_fusion
  14.4 0.0 collective-permute-done.2.refs_8_
  14.4 13.2 %collective-permute-done.1.refs_7_ = bf16[256,512]{1,0:T(8,128)(2,1)S(1)} collective-permute-done((bf16[256,512]{1,0:T(8,128)(2,1)}, bf16[256,512]{1,0:T(8,128)(2,1)S(1)}, u32[]{:S(2)}, u32[]{:S(2)}) %collective-permute-start.1) | collective-permute-done | bytes 262176 | tf_op jit(solution)/shard_map/ppermute | solution.py:245
  27.6 0.0 collective-permute-done.refs_6_
  27.6 0.0 copy-done
  27.6 0.0 copy-done.1
  27.6 12.5 %shard_map.74 = f32[256,256]{1,0:T(8,128)S(1)} custom-call(s32[8]{0:T(128)S(1)} %fusion.refs_0_, f32[8]{0:T(128)S(1)} %broadcast_select_fusion.refs_1_, bf16[256,512]{1,0:T(8,128)(2,1)S(1)} %get-tuple-element.7.refs_2_, bf16[256,512]{1,0:T(8,128)(2,1)S(1)} %get-tuple-element.8.refs_3_, f32[256,256]{1,0:T(8,128)S(1)} %copy-done, ...), custom_call_target="tpu_custom_call" | custom-call | tf_op jit(solution)/shard_map/pallas_call | solution.py:220
  40.0 0.7 %copy.10 = f32[256,256]{1,0:T(8,128)} copy(f32[256,256]{1,0:T(8,128)S(1)} %shard_map.74) | data formatting | bytes 524288
  (2 shorter events, 0.0 us)
Async XLA Ops:
  0.0 14.4 %collective-permute-start.2 = (bf16[256,512]{1,0:T(8,128)(2,1)}, bf16[256,512]{1,0:T(8,128)(2,1)S(1)}, u32[]{:S(2)}, u32[]{:S(2)}) collective-permute-start(bf16[256,512]{1,0:T(8,128)(2,1)} %bitcast.5), channel_id=1, source_target_pairs={{0,3},{1,0},{2,1},{3,2},{4,7},{5,4},{6,5},{7,6},{8,11},{9,8},{10,9... | collective-permute-start | bytes 786440 | tf_op jit(solution)/shard_map/ppermute | solution.py:245
  5.0 22.5 %collective-permute-start.1 = (bf16[256,512]{1,0:T(8,128)(2,1)}, bf16[256,512]{1,0:T(8,128)(2,1)S(1)}, u32[]{:S(2)}, u32[]{:S(2)}) collective-permute-start(bf16[256,512]{1,0:T(8,128)(2,1)} %bitcast.6), channel_id=1, source_target_pairs={{0,2},{1,3},{2,0},{3,1},{4,6},{5,7},{6,4},{7,5},{8,10},{9,11},{10,... | collective-permute-start | bytes 786440 | tf_op jit(solution)/shard_map/ppermute | solution.py:245
  5.1 22.5 %collective-permute-start = (bf16[256,512]{1,0:T(8,128)(2,1)}, bf16[256,512]{1,0:T(8,128)(2,1)S(1)}, u32[]{:S(2)}, u32[]{:S(2)}) collective-permute-start(bf16[256,512]{1,0:T(8,128)(2,1)} %bitcast.7), channel_id=1, source_target_pairs={{0,1},{1,2},{2,3},{3,0},{4,5},{5,6},{6,7},{7,4},{8,9},{9,10},{10,1... | collective-permute-start | bytes 786440 | tf_op jit(solution)/shard_map/ppermute | solution.py:245
  6.1 1.2 %copy-start.2 = (f32[1,512,512]{2,1,0:T(8,128)S(1)}, f32[1,512,512]{2,1,0:T(8,128)}, u32[]{:S(2)}) copy-start(f32[1,512,512]{2,1,0:T(8,128)} %param.7) | copy-start | bytes 3145732
  7.3 0.9 %copy-start.3 = (bf16[1,256,512]{2,1,0:T(8,128)(2,1)S(1)}, bf16[1,256,512]{2,1,0:T(8,128)(2,1)}, u32[]{:S(2)}) copy-start(bf16[1,256,512]{2,1,0:T(8,128)(2,1)} %param.9) | copy-start | bytes 786436
  8.3 19.3 %copy-start = (f32[256,256]{1,0:T(8,128)S(1)}, f32[256,256]{1,0:T(8,128)}, u32[]{:S(2)}) copy-start(f32[256,256]{1,0:T(8,128)} %refs_4_.1) | copy-start | bytes 786436
  8.3 19.3 %copy-start.1 = (bf16[1,256,512]{2,1,0:T(8,128)(2,1)S(1)}, bf16[1,256,512]{2,1,0:T(8,128)(2,1)}, u32[]{:S(2)}) copy-start(bf16[1,256,512]{2,1,0:T(8,128)(2,1)} %param.8) | copy-start | bytes 786436
  12.9 0.7 %copy-start.4 = (s32[8]{0:T(128)S(1)}, s32[8]{0:T(128)}, u32[]{:S(2)}) copy-start(s32[8]{0:T(128)} %param.12) | copy-start | bytes 100
  12.9 0.7 %copy-start.5 = (s32[1,4]{1,0:T(1,128)S(1)}, s32[1,4]{1,0:T(1,128)}, u32[]{:S(2)}) copy-start(s32[1,4]{1,0:T(1,128)} %param.10) | copy-start | bytes 52

commit v2 on v0

v2 whole, which is shorter than its diff:
```python
import functools

import jax
import jax.numpy as jnp
from jax import lax
from jax.experimental import pallas as pl
from jax.experimental.pallas import tpu as pltpu
from jax.sharding import PartitionSpec as P

F32 = jnp.float32
BF16 = jnp.bfloat16
MESH = pl.DeviceIdType.MESH
LEAST = 30.0
MOST = 64.0 * LEAST
NEWTON_STEPS = 3
REFINEMENTS = 3
CHUNKS = 4
VMEM_LIMIT = 56 * 1024 * 1024


def mm(a, b):
    return jnp.dot(a, b, preferred_element_type=F32)


def split(a):
    high = a.astype(BF16)
    return high, (a - high.astype(F32)).astype(BF16)


def eliminate(diag_ref, panel_ref, solved_ref, low_ref, sides_ref):
    n = diag_ref.shape[0]
    low_ref[...] = diag_ref[...]
    sides_ref[...] = panel_ref[...].astype(F32).T
    lane = lax.broadcasted_iota(jnp.int32, (1, n), 1)
    place = lax.broadcasted_iota(jnp.int32, (n, 1), 0)

    def pivot(k, carry):
        row = low_ref[pl.ds(k, 1), :]
        side = sides_ref[pl.ds(k, 1), :]
        scale = 1.0 / jnp.sum(jnp.where(lane == k, row, 0.0), axis=1, keepdims=True)
        col = jnp.sum(jnp.where(lane == k, low_ref[...], 0.0), axis=1, keepdims=True)
        col = jnp.where(place == k, 0.0, col)
        row, side = row * scale, side * scale
        low_ref[...] = low_ref[...] - col * row
        sides_ref[...] = sides_ref[...] - col * side
        low_ref[pl.ds(k, 1), :] = row
        sides_ref[pl.ds(k, 1), :] = side
        return carry

    lax.fori_loop(0, n, pivot, 0)
    solved_ref[...] = sides_ref[...].T


def direct_kernel(diag_ref, panel_ref, flag_ref, solved_ref, low_ref, sides_ref):
    most = jnp.max(jnp.sum(jnp.abs(diag_ref[...]), axis=1))
    wide_spectrum = jnp.logical_not(most <= MOST)
    flag_ref[0] = wide_spectrum.astype(jnp.int32)

    @pl.when(wide_spectrum)
    def _():
        eliminate(diag_ref, panel_ref, solved_ref, low_ref, sides_ref)


def direct(diag, panel):
    n, rows = diag.shape[0], panel.shape[0]
    vmem = pl.BlockSpec(memory_space=pltpu.VMEM)
    return pl.pallas_call(
        direct_kernel,
        out_shape=[jax.ShapeDtypeStruct((1,), jnp.int32), jax.ShapeDtypeStruct((rows, n), F32)],
        in_specs=[vmem, vmem],
        out_specs=[pl.BlockSpec(memory_space=pltpu.SMEM), vmem],
        scratch_shapes=[pltpu.VMEM((n, n), F32), pltpu.VMEM((n, rows), F32)],
        compiler_params=pltpu.CompilerParams(vmem_limit_bytes=VMEM_LIMIT),
    )(diag, panel)


def solve(diag_ref, panel_ref, e_ref, x_ref, y_ref):
    n = diag_ref.shape[0]
    diag = diag_ref[...]
    eye = (
        lax.broadcasted_iota(jnp.int32, (n, n), 0) == lax.broadcasted_iota(jnp.int32, (n, n), 1)
    ).astype(F32)
    scale = 2.0 / (LEAST + MOST)
    gap = (MOST - LEAST) / (MOST + LEAST)
    e = eye - scale * diag
    gain = 2.0 / (2.0 - gap * gap)
    x_ref[...] = (gain * scale) * (eye + e)
    eb = e.astype(BF16)
    e_ref[...] = (1.0 - gain) * eye + gain * mm(eb, eb)
    for _ in range(NEWTON_STEPS):
        gap = gap * gap * 0.5 * gain
        gain = 2.0 / (2.0 - gap * gap)
        eb = e_ref[...].astype(BF16)
        x = x_ref[...]
        x_ref[...] = gain * (x + mm(x.astype(BF16), eb))
        e_ref[...] = (1.0 - gain) * eye + gain * mm(eb, eb)
    x = x_ref[...]
    inverse = (x + mm(x.astype(BF16), e_ref[...].astype(BF16))).astype(BF16)
    panel = panel_ref[...]
    diag_high, diag_low = split(diag)
    y_ref[...] = mm(panel, inverse)
    for _ in range(REFINEMENTS):
        y = y_ref[...]
        y_high, y_low = split(y)
        rest = panel.astype(F32) - mm(y_high, diag_high) - mm(y_high, diag_low) - mm(y_low, diag_high)
        y_ref[...] = y + mm(rest.astype(BF16), inverse)


def update_kernel(
    wide, narrow,
    place_ref, weight_ref, flag_ref, solved_ref, diag_ref, panel_ref, row_ref, trailing_ref,
    out_ref,
    e_ref, x_ref, y_ref, gathered, products, acc, sends, recvs,
    gather_send, gather_recv, wide_send, wide_recv,
):
    bits = wide.bit_length() - 1
    size = out_ref.shape[0]
    part = size // CHUNKS
    me = lax.axis_index("wide")
    pos = lax.axis_index("narrow")
    own_bit = [lax.rem(lax.div(me, 1 << b), 2) for b in range(bits)]
    has_left, has_right = pos > 0, pos < narrow - 1

    def partner(b):
        return me + (1 - 2 * own_bit[b]) * (1 << b)

    def slot(r):
        return sum(
            ((1 - own_bit[b]) if (r >> b) & 1 else own_bit[b]) * (1 << b) for b in range(bits)
        )

    barrier = pltpu.get_barrier_semaphore()
    for b in range(bits):
        pl.semaphore_signal(barrier, inc=1, device_id={"wide": partner(b)}, device_id_type=MESH)
    for there, step in ((has_left, -1), (has_right, 1)):
        @pl.when(there)
        def _(step=step):
            pl.semaphore_signal(barrier, inc=1, device_id={"narrow": pos + step}, device_id_type=MESH)
    gathered[pos] = row_ref[...]
    pl.semaphore_wait(barrier, bits + has_left.astype(jnp.int32) + has_right.astype(jnp.int32))

    def pass_on(tile, c, step):
        block = gathered.at[tile, pl.ds(c * part, part)]
        return pltpu.make_async_remote_copy(
            src_ref=block,
            dst_ref=block,
            send_sem=gather_send.at[(step + 1) // 2, tile, c],
            recv_sem=gather_recv.at[tile, c],
            device_id={"narrow": pos + step},
            device_id_type=MESH,
        )

    for c in range(CHUNKS):
        for there, step in ((has_left, -1), (has_right, 1)):
            @pl.when(there)
            def _(c=c, step=step):
                pass_on(pos, c, step).start()

    solve(diag_ref, panel_ref, e_ref, x_ref, y_ref)
    y = jnp.where(flag_ref[0] > 0, solved_ref[...], y_ref[...])
    high, low = split(y)
    dims = (((1,), (1,)), ((), ()))

    def gather(c):
        for d in range(1, narrow):
            @pl.when(pos >= d)
            def _(d=d):
                pass_on(pos - d, c, -1).wait_recv()

                @pl.when(has_right)
                def _():
                    pass_on(pos - d, c, 1).start()

            @pl.when(pos + d < narrow)
            def _(d=d):
                pass_on(pos + d, c, 1).wait_recv()

                @pl.when(has_left)
                def _():
                    pass_on(pos + d, c, -1).start()

    orders = [
        [0] + (list(range(1, bits)) if c % 2 == 0 else list(range(bits - 1, 0, -1)))
        for c in range(CHUNKS)
    ]
    left = [list(range(wide)) for _ in range(CHUNKS)]
    bases = [0] * CHUNKS
    waiting = [None] * CHUNKS

    def exchange(c, s, value):
        b = orders[c][s]
        gone = [r for r in left[c] if (r >> b) & 1]
        left[c] = [r for r in left[c] if not (r >> b) & 1]
        at, count = bases[c], len(gone)
        bases[c] = at + count
        for i, r in enumerate(gone):
            sends[c, at + i] = value(r).astype(BF16)
        copy = pltpu.make_async_remote_copy(
            src_ref=sends.at[c, pl.ds(at, count)],
            dst_ref=recvs.at[c, pl.ds(at, count)],
            send_sem=wide_send.at[c, s],
            recv_sem=wide_recv.at[c, s],
            device_id={"wide": partner(b)},
            device_id_type=MESH,
        )
        copy.start()
        waiting[c] = (copy, {r - (1 << b): at + i for i, r in enumerate(gone)})

    def multiply(c):
        rows = gathered[:, c * part : (c + 1) * part, :].reshape(narrow * part, row_ref.shape[1])
        result = lax.dot_general(rows, high, dims, preferred_element_type=F32) + lax.dot_general(
            rows, low, dims, preferred_element_type=F32
        )
        products[c] = result.reshape(narrow, part, size)
        exchange(c, 0, lambda r: own(c, r))

    def own(c, r):
        p = slot(r)
        return products[c, place_ref[p]] * weight_ref[p]

    def collect(c, s):
        copy, found = waiting[c]
        copy.wait()
        for r in left[c]:
            held = own(c, r) if s == 0 else acc[c, r]
            acc[c, r] = held + recvs[c, found[r]].astype(F32)
        if s + 1 < bits:
            exchange(c, s + 1, lambda r: acc[c, r])
        else:
            rows = slice(c * part, (c + 1) * part)
            out_ref[rows, :] = trailing_ref[rows, :] - acc[c, 0]

    for turn in range(CHUNKS + bits):
        if turn < CHUNKS:
            gather(turn)
            multiply(turn)
        for s in range(bits):
            c = turn - 1 - s
            if 0 <= c < CHUNKS:
                collect(c, s)

    for c in range(CHUNKS):
        for d in range(narrow):
            @pl.when(has_right & (pos >= d))
            def _(c=c, d=d):
                pass_on(pos - d, c, 1).wait_send()

            @pl.when(has_left & (pos + d < narrow))
            def _(c=c, d=d):
                pass_on(pos + d, c, -1).wait_send()


def update(wide, narrow, place, weight, flag, solved, diag, panel, row_panel, trailing):
    rows, cols = trailing.shape
    n = diag.shape[0]
    part = rows // CHUNKS
    bits = wide.bit_length() - 1
    vmem = pl.BlockSpec(memory_space=pltpu.VMEM)
    smem = pl.BlockSpec(memory_space=pltpu.SMEM)
    return pl.pallas_call(
        functools.partial(update_kernel, wide, narrow),
        out_shape=jax.ShapeDtypeStruct((rows, cols), F32),
        in_specs=[smem] * 3 + [vmem] * 5,
        out_specs=vmem,
        scratch_shapes=[
            pltpu.VMEM((n, n), F32),
            pltpu.VMEM((n, n), F32),
            pltpu.VMEM((panel.shape[0], n), F32),
            pltpu.VMEM((narrow,) + row_panel.shape, BF16),
            pltpu.VMEM((CHUNKS, narrow, part, cols), F32),
            pltpu.VMEM((CHUNKS, wide, part, cols), F32),
            pltpu.VMEM((CHUNKS, wide - 1, part, cols), BF16),
            pltpu.VMEM((CHUNKS, wide - 1, part, cols), BF16),
            pltpu.SemaphoreType.DMA((2, narrow, CHUNKS)),
            pltpu.SemaphoreType.DMA((narrow, CHUNKS)),
            pltpu.SemaphoreType.DMA((CHUNKS, bits)),
            pltpu.SemaphoreType.DMA((CHUNKS, bits)),
        ],
        compiler_params=pltpu.CompilerParams(
            collective_id=0, has_side_effects=True, vmem_limit_bytes=VMEM_LIMIT
        ),
    )(place, weight, flag, solved, diag, panel, row_panel, trailing)


def local(wide, narrow, diag_blocks, row_panel, col_panel, row_tiles, col_mask, slot_tile, trailing):
    flag, solved = direct(diag_blocks[0], col_panel[0])
    hits = slot_tile[:, None] == row_tiles[0][None, :]
    tile = jnp.arange(narrow, dtype=jnp.int32)
    place = jnp.sum(jnp.where(hits, tile[None, :], 0), axis=1).astype(jnp.int32)
    weight = jnp.any(hits, axis=1).astype(F32) * col_mask[0, 0].astype(F32)
    return update(
        wide, narrow, place, weight, flag, solved, diag_blocks[0], col_panel[0], row_panel[0], trailing
    )


def solution(mesh):
    placed = (
        P("wide", None, None),
        P("wide", "narrow", None),
        P("wide", "narrow", None),
        P("wide", None),
        P("wide", "narrow"),
        P(),
        P("wide", "narrow"),
    )
    return jax.shard_map(
        functools.partial(local, mesh.shape["wide"], mesh.shape["narrow"]),
        mesh=mesh,
        in_specs=placed,
        out_specs=P("wide", "narrow"),
        check_vma=False,
    )
```

time: 226 us -> 46.3 us (0.20)
  other arithmetic: 121 us -> 1.26 us
  waiting for transfers between devices: 63.5 us -> 0 us
  Pallas kernels: 0 us -> 41.8 us
  between operations: 16.9 us -> 0.69 us
  matrix products: 11.4 us -> 0 us
  local copies, waits for them, and re-layouts: 12.6 us -> 2.33 us
    another operation x18 -> x0, other arithmetic: 118 us -> none  [the longest x14 78.6 us: local(): factor_low = jax.vmap(jnp.linalg.cholesky)(diag_blocks)]
    pallas_call x0 -> x2, Pallas kernels: none -> 41.8 us  [the longest x1 39.5 us: update(): pl.pallas_call(functools.partial(update_kernel, wide, narrow), out_shape=...]
    reduce_scatter x1 -> x0, waiting for transfers between devices: 34.5 us -> none  [local(): lax.psum_scatter(gathered_sum.reshape(slot_count * tile_rows, tile_rows)....]
    all_gather x1 -> x0, waiting for transfers between devices: 29 us -> none  [local(): lax.all_gather(row_factor, 'narrow', axis=1, tiled=True)]
    another operation x18 -> x0, local copies, waits for them, and re-layouts: 9.69 us -> none  [the longest x13 8.06 us: solve_single(): lax.linalg.triangular_solve(factor_low, panel.astype(jnp.float32), left_s...]
    another operation x20 -> x0, matrix products: 8.01 us -> none  [the longest x14 6.13 us: solve_single(): lax.linalg.triangular_solve(factor_low, panel.astype(jnp.float32), left_s...]
    dot_general x3 -> x0, matrix products: 3.44 us -> none  [the longest x1 2.81 us: local(): jnp.einsum('sap,saij->pij', placing, blocks, precision=lax.Precision.HIGH...]
  transfers between devices with their start and end apart: 2 -> 0, of which waited for: 2 -> 0; matrix products, arithmetic and copies ran while one was open for 1% -> 0% of each run, Pallas kernels for 0% -> 0%
where the time goes in v2:
time: 46.3 us; the launch traced here: 46.1 us
  Pallas kernels  41.8 us (90%)
  local copies, waits for them, and re-layouts  2.33 us (5%)
  other arithmetic  1.26 us (3%)
  between operations  0.69 us (1%)
    pallas_call x1, Pallas kernels, update(): pl.pallas_call(functools.partial(update_kernel, wide, narrow), out_shape=...  39.5 us
    pallas_call x1, Pallas kernels, direct(): pl.pallas_call(direct_kernel, out_shape=[jax.ShapeDtypeStruct((1,), jnp.i...  2.33 us
    unnamed x5, local copies, waits for them, and re-layouts  2.33 us

profile of v2, /device:TPU:0, one launch (start us, length us, event | category | flops | bytes accessed | tf_op | source)
XLA Modules:
  0.0 46.1 jit_solution(5930396580468245998)
XLA Ops:
  0.7 0.0 copy-start
  0.7 0.0 copy-start.1
  0.7 0.6 %copy-done = s32[8]{0:T(128)S(1)} copy-done((s32[8]{0:T(128)S(1)}, s32[8]{0:T(128)}, u32[]{:S(2)}) %copy-start) | copy-done | bytes 56
  1.3 0.0 copy-done.1
  1.3 0.1 compare_reduce_fusion
  1.4 0.6 %broadcast_select_fusion.weight_ref = f32[8]{0:T(128)} fusion(pred[8]{0:T(512)(128)(4,1)S(1)} %compare_reduce_fusion, f32[]{:T(128)} %bitcast.1), kind=kLoop, calls=%fused_computation.3 | loop fusion | flops 8 | bytes 44 | tf_op jit(solution)/shard_map/mul | solution.py:290
  2.0 0.6 %fusion.place_ref = s32[8]{0:T(128)} fusion(s32[8]{0:T(128)S(1)} %copy-done, s32[4]{0:T(128)S(1)} %bitcast.11), kind=kLoop, calls=%fused_computation.2 | loop fusion | flops 88 | bytes 80 | tf_op jit(solution)/shard_map/reduce_sum | solution.py:289
  2.6 2.3 %shard_map.73 = (s32[1]{0:T(128)}, f32[256,512]{1,0:T(8,128)}) custom-call(f32[512,512]{1,0:T(8,128)} %bitcast.5, bf16[256,512]{1,0:T(8,128)(2,1)} %bitcast.7), custom_call_target="tpu_custom_call" | custom-call | tf_op jit(solution)/shard_map/pallas_call | solution.py:67
  4.9 39.5 %shard_map.74 = f32[256,256]{1,0:T(8,128)} custom-call(s32[8]{0:T(128)} %fusion.place_ref, f32[8]{0:T(128)} %broadcast_select_fusion.weight_ref, s32[1]{0:T(128)} %get-tuple-element.7.flag_ref, f32[256,512]{1,0:T(8,128)} %get-tuple-element.8.solved_ref, f32[512,512]{1,0:T(8,128)} %bitcast.6, bf16[256,512]{1,0:T(8,128)(2,1)} %bitcast.8, ...), custom_call_target="tpu_custom_call" | custom-call | tf_op jit(solution)/shard_map/pallas_call | solution.py:260
  44.5 1.7 %copy.10 = f32[256,256]{1,0:T(8,128)} copy(f32[256,256]{1,0:T(8,128)} %shard_map.74) | data formatting | bytes 524288
Async XLA Ops:
  0.7 0.7 %copy-start = (s32[8]{0:T(128)S(1)}, s32[8]{0:T(128)}, u32[]{:S(2)}) copy-start(s32[8]{0:T(128)} %param.12) | copy-start | bytes 100
  0.7 0.7 %copy-start.1 = (s32[1,4]{1,0:T(1,128)S(1)}, s32[1,4]{1,0:T(1,128)}, u32[]{:S(2)}) copy-start(s32[1,4]{1,0:T(1,128)} %param.10) | copy-start | bytes 52

commit v3 on v2

--- a/solution.py
+++ b/solution.py
@@ -15,7 +15,6 @@
 NEWTON_STEPS = 3
 REFINEMENTS = 3
 CHUNKS = 4
-VMEM_LIMIT = 56 * 1024 * 1024
 
 
 def mm(a, b):
@@ -70,11 +69,11 @@
         in_specs=[vmem, vmem],
         out_specs=[pl.BlockSpec(memory_space=pltpu.SMEM), vmem],
         scratch_shapes=[pltpu.VMEM((n, n), F32), pltpu.VMEM((n, rows), F32)],
-        compiler_params=pltpu.CompilerParams(vmem_limit_bytes=VMEM_LIMIT),
+        compiler_params=pltpu.CompilerParams(vmem_limit_bytes=16 * 1024 * 1024),
     )(diag, panel)
 
 
-def solve(diag_ref, panel_ref, e_ref, x_ref, y_ref):
+def solve(diag_ref, panel_ref, e_ref, x_ref, y_ref, between):
     n = diag_ref.shape[0]
     diag = diag_ref[...]
     eye = (
@@ -94,12 +93,14 @@
         x = x_ref[...]
         x_ref[...] = gain * (x + mm(x.astype(BF16), eb))
         e_ref[...] = (1.0 - gain) * eye + gain * mm(eb, eb)
+    between(0)
     x = x_ref[...]
     inverse = (x + mm(x.astype(BF16), e_ref[...].astype(BF16))).astype(BF16)
     panel = panel_ref[...]
     diag_high, diag_low = split(diag)
     y_ref[...] = mm(panel, inverse)
-    for _ in range(REFINEMENTS):
+    for turn in range(REFINEMENTS):
+        between(turn + 1)
         y = y_ref[...]
         y_high, y_low = split(y)
         rest = panel.astype(F32) - mm(y_high, diag_high) - mm(y_high, diag_low) - mm(y_low, diag_high)
@@ -108,7 +109,7 @@
 
 def update_kernel(
     wide, narrow,
-    place_ref, weight_ref, flag_ref, solved_ref, diag_ref, panel_ref, row_ref, trailing_ref,
+    row_tiles_ref, mask_ref, slot_tile_ref, flag_ref, solved_ref, diag_ref, panel_ref, row_ref, trailing_ref,
     out_ref,
     e_ref, x_ref, y_ref, gathered, products, acc, sends, recvs,
     gather_send, gather_recv, wide_send, wide_recv,
@@ -129,6 +130,15 @@
             ((1 - own_bit[b]) if (r >> b) & 1 else own_bit[b]) * (1 << b) for b in range(bits)
         )
 
+    placing = []
+    for r in range(wide):
+        held = slot_tile_ref[slot(r)]
+        tile = found = jnp.int32(0)
+        for t in range(narrow):
+            hit = row_tiles_ref[0, t] == held
+            tile, found = jnp.where(hit, t, tile), jnp.where(hit, 1, found)
+        placing.append((tile, (found * mask_ref[0, 0]).astype(F32)))
+
     barrier = pltpu.get_barrier_semaphore()
     for b in range(bits):
         pl.semaphore_signal(barrier, inc=1, device_id={"wide": partner(b)}, device_id_type=MESH)
@@ -156,28 +166,34 @@
             def _(c=c, step=step):
                 pass_on(pos, c, step).start()
 
-    solve(diag_ref, panel_ref, e_ref, x_ref, y_ref)
+    def gather(c, distances):
+        for d in distances:
+            @pl.when(pos >= d)
+            def _(d=d):
+                pass_on(pos - d, c, -1).wait_recv()
+
+                @pl.when(has_right)
+                def _():
+                    pass_on(pos - d, c, 1).start()
+
+            @pl.when(pos + d < narrow)
+            def _(d=d):
+                pass_on(pos + d, c, 1).wait_recv()
+
+                @pl.when(has_left)
+                def _():
+                    pass_on(pos + d, c, -1).start()
+
+    def near(c):
+        if c < CHUNKS:
+            gather(c, [1])
+
+    solve(diag_ref, panel_ref, e_ref, x_ref, y_ref, near)
+    for c in range(REFINEMENTS + 1, CHUNKS):
+        near(c)
     y = jnp.where(flag_ref[0] > 0, solved_ref[...], y_ref[...])
     high, low = split(y)
     dims = (((1,), (1,)), ((), ()))
-
-    def gather(c):
-        for d in range(1, narrow):
-            @pl.when(pos >= d)
-            def _(d=d):
-                pass_on(pos - d, c, -1).wait_recv()
-
-                @pl.when(has_right)
-                def _():
-                    pass_on(pos - d, c, 1).start()
-
-            @pl.when(pos + d < narrow)
-            def _(d=d):
-                pass_on(pos + d, c, 1).wait_recv()
-
-                @pl.when(has_left)
-                def _():
-                    pass_on(pos + d, c, -1).start()
 
     orders = [
         [0] + (list(range(1, bits)) if c % 2 == 0 else list(range(bits - 1, 0, -1)))
@@ -215,8 +231,8 @@
         exchange(c, 0, lambda r: own(c, r))
 
     def own(c, r):
-        p = slot(r)
-        return products[c, place_ref[p]] * weight_ref[p]
+        tile, weight = placing[r]
+        return products[c, tile] * weight
 
     def collect(c, s):
         copy, found = waiting[c]
@@ -232,7 +248,7 @@
 
     for turn in range(CHUNKS + bits):
         if turn < CHUNKS:
-            gather(turn)
+            gather(turn, range(2, narrow))
             multiply(turn)
         for s in range(bits):
             c = turn - 1 - s
@@ -250,17 +266,19 @@
                 pass_on(pos + d, c, -1).wait_send()
 
 
-def update(wide, narrow, place, weight, flag, solved, diag, panel, row_panel, trailing):
+def update(wide, narrow, row_tiles, mask, slot_tile, flag, solved, diag, panel, row_panel, trailing):
     rows, cols = trailing.shape
     n = diag.shape[0]
     part = rows // CHUNKS
     bits = wide.bit_length() - 1
     vmem = pl.BlockSpec(memory_space=pltpu.VMEM)
     smem = pl.BlockSpec(memory_space=pltpu.SMEM)
+    tile = rows * cols * 4
+    scratch = (2 * n * n + panel.shape[0] * n) * 4 + narrow * row_panel.size * 2 + tile * (narrow + 2 * wide)
     return pl.pallas_call(
         functools.partial(update_kernel, wide, narrow),
         out_shape=jax.ShapeDtypeStruct((rows, cols), F32),
-        in_specs=[smem] * 3 + [vmem] * 5,
+        in_specs=[smem] * 4 + [vmem] * 5,
         out_specs=vmem,
         scratch_shapes=[
             pltpu.VMEM((n, n), F32),
@@ -277,19 +295,16 @@
             pltpu.SemaphoreType.DMA((CHUNKS, bits)),
         ],
         compiler_params=pltpu.CompilerParams(
-            collective_id=0, has_side_effects=True, vmem_limit_bytes=VMEM_LIMIT
+            collective_id=0, has_side_effects=True, vmem_limit_bytes=scratch + 18 * 1024 * 1024
         ),
-    )(place, weight, flag, solved, diag, panel, row_panel, trailing)
+    )(row_tiles, mask, slot_tile, flag, solved, diag, panel, row_panel, trailing)
 
 
 def local(wide, narrow, diag_blocks, row_panel, col_panel, row_tiles, col_mask, slot_tile, trailing):
-    flag, solved = direct(diag_blocks[0], col_panel[0])
-    hits = slot_tile[:, None] == row_tiles[0][None, :]
-    tile = jnp.arange(narrow, dtype=jnp.int32)
-    place = jnp.sum(jnp.where(hits, tile[None, :], 0), axis=1).astype(jnp.int32)
-    weight = jnp.any(hits, axis=1).astype(F32) * col_mask[0, 0].astype(F32)
+    diag, panel = diag_blocks[0], col_panel[0]
+    flag, solved = direct(diag, panel)
     return update(
-        wide, narrow, place, weight, flag, solved, diag_blocks[0], col_panel[0], row_panel[0], trailing
+        wide, narrow, row_tiles, col_mask, slot_tile, flag, solved, diag, panel, row_panel[0], trailing
     )
 
 

time: 46.3 us -> 42.6 us (0.920)
  Pallas kernels: 41.8 us -> 36.1 us
  local copies, waits for them, and re-layouts: 2.33 us -> 5.53 us
  other arithmetic: 1.26 us -> 0 us
    pallas_call x1, Pallas kernels: 39.5 us -> 35.3 us  [update(): pl.pallas_call(functools.partial(update_kernel, wide, narrow), out_shape=...]
    unnamed x5 -> x17, local copies, waits for them, and re-layouts: 2.33 us -> 5.53 us
    pallas_call x1, Pallas kernels: 2.33 us -> 0.78 us  [direct(): pl.pallas_call(direct_kernel, out_shape=[jax.ShapeDtypeStruct((1,), jnp.i...]
    reduce_sum x1 -> x0, other arithmetic: 0.59 us -> none  [local(): place = jnp.sum(jnp.where(hits, tile[None, :], 0), axis=1).astype(jnp.int32)]
    mul x1 -> x0, other arithmetic: 0.58 us -> none  [local(): weight = jnp.any(hits, axis=1).astype(F32) * col_mask[0, 0].astype(F32)]
where the time goes in v3:
time: 42.6 us; the launch traced here: 42.3 us
  Pallas kernels  36.1 us (85%)
  local copies, waits for them, and re-layouts  5.53 us (13%)
  between operations  0.7 us (2%)
    pallas_call x1, Pallas kernels, update(): pl.pallas_call(functools.partial(update_kernel, wide, narrow), out_shape=...  35.3 us
    unnamed x17, local copies, waits for them, and re-layouts  5.53 us

profile of v3, /device:TPU:0, one launch (start us, length us, event | category | flops | bytes accessed | tf_op | source)
XLA Modules:
  0.0 42.3 jit_solution(14468486806256460478)
XLA Ops:
  0.7 0.0 copy-start
  0.7 1.2 %copy-done = f32[1,512,512]{2,1,0:T(8,128)S(1)} copy-done((f32[1,512,512]{2,1,0:T(8,128)S(1)}, f32[1,512,512]{2,1,0:T(8,128)}, u32[]{:S(2)}) %copy-start) | copy-done | bytes 1048600
  1.9 0.0 copy-start.2
  1.9 0.9 %copy-done.2 = bf16[1,256,512]{2,1,0:T(8,128)(2,1)S(1)} copy-done((bf16[1,256,512]{2,1,0:T(8,128)(2,1)S(1)}, bf16[1,256,512]{2,1,0:T(8,128)(2,1)}, u32[]{:S(2)}) %copy-start.2) | copy-done | bytes 262168
  2.8 0.0 copy-start.1
  2.8 0.0 copy-start.3
  2.8 0.8 %shard_map.73 = (s32[1]{0:T(128)}, f32[256,512]{1,0:T(8,128)S(1)}) custom-call(f32[512,512]{1,0:T(8,128)S(1)} %bitcast.3, bf16[256,512]{1,0:T(8,128)(2,1)S(1)} %bitcast.5), custom_call_target="tpu_custom_call" | custom-call | tf_op jit(solution)/shard_map/pallas_call | solution.py:66
  3.6 0.0 copy-start.6
  3.6 0.0 copy-start.7
  3.6 0.4 copy-done.1
  4.1 0.0 copy-done.3
  4.1 0.3 copy-done.6
  4.4 0.0 copy-done.7
  4.4 0.0 copy-start.4
  4.4 0.9 %copy-done.4 = bf16[1,256,512]{2,1,0:T(8,128)(2,1)S(1)} copy-done((bf16[1,256,512]{2,1,0:T(8,128)(2,1)S(1)}, bf16[1,256,512]{2,1,0:T(8,128)(2,1)}, u32[]{:S(2)}) %copy-start.4) | copy-done | bytes 262168
  5.3 0.0 copy-start.5
  5.3 0.9 %copy-done.5 = f32[256,256]{1,0:T(8,128)S(1)} copy-done((f32[256,256]{1,0:T(8,128)S(1)}, f32[256,256]{1,0:T(8,128)}, u32[]{:S(2)}) %copy-start.5) | copy-done | bytes 262168
  6.3 35.3 %shard_map.74 = f32[256,256]{1,0:T(8,128)S(1)} custom-call(s32[1,4]{1,0:T(1,128)S(1)} %copy-done.6, s32[1,1]{1,0:T(1,128)S(6)} %copy.9.mask_ref, s32[8]{0:T(128)S(1)} %copy-done.7, s32[1]{0:T(128)} %get-tuple-element.7.flag_ref, f32[256,512]{1,0:T(8,128)S(1)} %get-tuple-element.8.solved_ref, f32[512,512]{1,0:T(8,128)S(1)} %bitcast.4, ...), custom_call_target="tpu_custom_call" | custom-call | tf_op jit(solution)/shard_map/pallas_call | solution.py:278
  41.6 0.7 %copy.10 = f32[256,256]{1,0:T(8,128)} copy(f32[256,256]{1,0:T(8,128)S(1)} %shard_map.74) | data formatting | bytes 524288
Async XLA Ops:
  0.7 1.2 %copy-start = (f32[1,512,512]{2,1,0:T(8,128)S(1)}, f32[1,512,512]{2,1,0:T(8,128)}, u32[]{:S(2)}) copy-start(f32[1,512,512]{2,1,0:T(8,128)} %param.7) | copy-start | bytes 3145732
  1.9 0.9 %copy-start.2 = (bf16[1,256,512]{2,1,0:T(8,128)(2,1)S(1)}, bf16[1,256,512]{2,1,0:T(8,128)(2,1)}, u32[]{:S(2)}) copy-start(bf16[1,256,512]{2,1,0:T(8,128)(2,1)} %param.9) | copy-start | bytes 786436
  2.8 1.2 %copy-start.1 = (f32[1,512,512]{2,1,0:T(8,128)S(1)}, f32[1,512,512]{2,1,0:T(8,128)}, u32[]{:S(2)}) copy-start(f32[1,512,512]{2,1,0:T(8,128)} %param.7) | copy-start | bytes 3145732
  2.8 1.3 %copy-start.3 = (bf16[1,256,512]{2,1,0:T(8,128)(2,1)S(1)}, bf16[1,256,512]{2,1,0:T(8,128)(2,1)}, u32[]{:S(2)}) copy-start(bf16[1,256,512]{2,1,0:T(8,128)(2,1)} %param.9) | copy-start | bytes 786436
  3.6 0.8 %copy-start.6 = (s32[1,4]{1,0:T(1,128)S(1)}, s32[1,4]{1,0:T(1,128)}, u32[]{:S(2)}) copy-start(s32[1,4]{1,0:T(1,128)} %row_tiles_ref.1) | copy-start | bytes 52
  3.6 0.8 %copy-start.7 = (s32[8]{0:T(128)S(1)}, s32[8]{0:T(128)}, u32[]{:S(2)}) copy-start(s32[8]{0:T(128)} %slot_tile_ref.1) | copy-start | bytes 100
  4.4 0.9 %copy-start.4 = (bf16[1,256,512]{2,1,0:T(8,128)(2,1)S(1)}, bf16[1,256,512]{2,1,0:T(8,128)(2,1)}, u32[]{:S(2)}) copy-start(bf16[1,256,512]{2,1,0:T(8,128)(2,1)} %param.8) | copy-start | bytes 786436
  5.3 0.9 %copy-start.5 = (f32[256,256]{1,0:T(8,128)S(1)}, f32[256,256]{1,0:T(8,128)}, u32[]{:S(2)}) copy-start(f32[256,256]{1,0:T(8,128)} %trailing_ref.1) | copy-start | bytes 786436
